TPU v7x, 256 devices: a whole 4x4x8 slice. The times are simulated.
256 devices in a mesh: dp: 128 (over y_lo, z, x, core), section: 2 (over y_hi).
Axes of the slice: x: 4, y: 4 (y_hi: 2, y_lo: 2; y = y_hi * 2 + y_lo), z: 8, core: 2. Of those that a mesh axis runs over, the one named last changes fastest.
Arguments:
- teacher_image: bfloat16 [65536, 1536], P(('dp', 'section')), may hold values from -6 to 6
- teacher_proj: bfloat16 [1536, 1536], replicated, may hold values from -0.15625 to 0.15625
- teacher_text: bfloat16 [65536, 1536], P(('dp', 'section')), may hold values from -6 to 6
- image_feats: bfloat16 [65536, 768], P(('dp', 'section')), may hold values from -6 to 6
- text_feats: bfloat16 [65536, 768], P(('dp', 'section')), may hold values from -6 to 6
- image_proj: bfloat16 [768, 768], replicated, may hold values from -0.21875 to 0.21875
- text_proj: bfloat16 [768, 768], replicated, may hold values from -0.21875 to 0.21875
- class_ids: int32 [65536], P(('dp', 'section')), may hold values from 0 to 255
Outputs:
- grad_image_proj: float32 [768, 768], replicated
- grad_text_proj: float32 [768, 768], replicated
All inputs are finite; a program needn't handle non-finite values.
Results may differ from a plain program's by a relative error of at most 0.005.
Values may be sent and summed in bfloat16 or wider, within the bound.
No kernel may reach another device: no remote copies, remote signals or barrier semaphores. Data moves between devices by JAX's collectives and lax.ppermute only.
A program may use at most 128 MiB of HBM per device.

v0:
```python
import jax
import jax.numpy as jnp
from jax import lax
from jax.sharding import PartitionSpec as P

WINDOW = 4
epsilon = 1e-06
teacher_scale = 20.0
teacher_shift = -1.0
student_scale = 20.0
student_shift = -1.0


def passed_along(block, axis, distance):
    devices = range(lax.axis_size(axis))
    route = [((i - distance) % len(devices), i) for i in devices]
    return lax.ppermute(block, axis, route)


def unit_rows(raw_rows):
    row_len = jnp.sqrt(jnp.sum(raw_rows * raw_rows, axis=1, keepdims=True) + epsilon)
    return (raw_rows / row_len, row_len)


def pair_tile(teach_rows, image_rows, row_ids, teach_cols, text_cols, col_ids):
    teacher_dot = lax.dot_general(
        teach_rows, teach_cols, (((1,), (1,)), ((), ())), preferred_element_type=jnp.float32
    )
    labels = (row_ids[:, None] == col_ids[None, :]).astype(jnp.float32)
    target = 0.5 * jax.nn.sigmoid(teacher_scale * teacher_dot + teacher_shift) + 0.5 * labels
    logits = (
        student_scale
        * lax.dot_general(
            image_rows, text_cols, (((1,), (1,)), ((), ())), preferred_element_type=jnp.float32
        )
        + student_shift
    )
    scaled = ((jax.nn.sigmoid(logits) - target) / text_cols.shape[0]).astype(jnp.bfloat16)
    row_part = student_scale * jnp.dot(scaled, text_cols, preferred_element_type=jnp.float32)
    col_part = student_scale * lax.dot_general(
        scaled, image_rows, (((0,), (0,)), ((), ())), preferred_element_type=jnp.float32
    )
    return (row_part, col_part)


def weight_grad(feats, unit, length, grad):
    direction = (grad - unit * jnp.sum(unit * grad, axis=1, keepdims=True)) / length
    high = direction.astype(jnp.bfloat16)
    low = (direction - high.astype(jnp.float32)).astype(jnp.bfloat16)
    dims = (((0,), (0,)), ((), ()))
    first = lax.dot_general(feats, high, dims, preferred_element_type=jnp.float32)
    second = lax.dot_general(feats, low, dims, preferred_element_type=jnp.float32)
    return first + second


def local(
    teacher_image,
    teacher_proj,
    teacher_text,
    image_feats,
    text_feats,
    image_proj,
    text_proj,
    class_ids,
):
    teacher_unit, teacher_len = unit_rows(
        jnp.dot(teacher_image, teacher_proj, preferred_element_type=jnp.float32)
    )
    teacher_img = teacher_unit.astype(jnp.bfloat16)
    written_unit, written_len = unit_rows(teacher_text.astype(jnp.float32))
    teacher_txt = written_unit.astype(jnp.bfloat16)
    own_ids = class_ids.astype(jnp.bfloat16)
    image_unit, image_len = unit_rows(
        jnp.dot(image_feats, image_proj, preferred_element_type=jnp.float32)
    )
    image_emb = image_unit.astype(jnp.bfloat16)
    teach_rows, image_rows, row_ids = (
        lax.all_gather(teacher_img, "section", axis=0, tiled=True),
        lax.all_gather(image_emb, "section", axis=0, tiled=True),
        lax.all_gather(own_ids, "section", axis=0, tiled=True),
    )
    grad_rows = jnp.zeros((image_rows.shape[0], image_rows.shape[1]), jnp.float32)
    text_unit, text_len = unit_rows(
        jnp.dot(text_feats, text_proj, preferred_element_type=jnp.float32)
    )
    text_emb = text_unit.astype(jnp.bfloat16)
    panels = (teacher_txt, text_emb, own_ids)
    carried = jnp.zeros(text_unit.shape, jnp.float32)
    for offset in range(WINDOW):
        if offset > 0:
            panels = passed_along((panels[0], panels[1], panels[2]), "dp", 1)
            carried = passed_along(carried, "dp", 1)
        row_part, col_part = pair_tile(
            teach_rows, image_rows, row_ids, panels[0], panels[1], panels[2]
        )
        grad_rows = grad_rows + row_part
        carried = carried + col_part
    grad_txt = passed_along(carried, "dp", 1 - WINDOW)
    text_part = weight_grad(text_feats, text_unit, text_len, grad_txt)
    own_grads = lax.psum_scatter(
        grad_rows.astype(jnp.bfloat16), "section", scatter_dimension=0, tiled=True
    ).astype(jnp.float32)
    image_part = weight_grad(image_feats, image_unit, image_len, own_grads)
    image_total, text_total = lax.psum((image_part, text_part), ("dp", "section"))
    return (image_total, text_total)


def solution(mesh):
    in_specs = (
        P(("dp", "section"), None),
        P(),
        P(("dp", "section"), None),
        P(("dp", "section"), None),
        P(("dp", "section"), None),
        P(),
        P(),
        P(("dp", "section")),
    )
    out_specs = (P(), P())
    return jax.shard_map(local, mesh=mesh, in_specs=in_specs, out_specs=out_specs, check_vma=False)
```

profile of v0, /device:TPU:2, one launch (start us, length us, event | category | flops | bytes accessed | tf_op | source)
XLA Modules:
  0.0 433.6 jit_solution(15911521493191360860)
XLA Ops:
  7.2 4.1 multiply_reduce_fusion
  14.1 1.6 collective-permute-start.1
  17.2 12.8 %collective-permute-done = bf16[256,768]{1,0:T(8,128)(2,1)} collective-permute-done((bf16[256,768]{1,0:T(8,128)(2,1)S(1)}, bf16[256,768]{1,0:T(8,128)(2,1)}, u32[]{:S(2)}, u32[]{:S(2)}) %collective-permute-start) | collective-permute-done | bytes 393248 | tf_op jit(solution)/shard_map/ppermute | solution.py:17
  30.1 22.3 %all_gather.9 = bf16[512,768]{1,0:T(8,128)(2,1)S(1)} all-gather(bf16[256,768]{1,0:T(8,128)(2,1)S(1)} %fusion.74), channel_id=1, replica_groups=mesh['dp'=128,'section'=2] {'section'}, dimensions={0}, use_global_device_ids=true | all-gather | bytes 1179648 | tf_op jit(solution)/shard_map/all_gather | solution.py:79
  54.5 5.7 %all-gather = bf16[2,1,256]{2,1,0:T(2,128)(2,1)S(1)} all-gather(bf16[1,1,256]{2,1,0:T(2,128)(2,1)S(1)} %reshape.35), channel_id=1, replica_groups=mesh['dp'=128,'section'=2] {'section'}, dimensions={0}, use_global_device_ids=true | all-gather | bytes 1536 | tf_op jit(solution)/shard_map/all_gather | solution.py:80
  61.8 2.4 fusion.62
  64.7 3.1 collective-permute-start.9
  68.2 1.8 fusion.43
  70.0 4.9 %collective-permute-done.4 = bf16[256,1536]{1,0:T(8,128)(2,1)} collective-permute-done((bf16[256,1536]{1,0:T(8,128)(2,1)}, bf16[256,1536]{1,0:T(8,128)(2,1)}, u32[]{:S(2)}, u32[]{:S(2)}) %collective-permute-start.4) | collective-permute-done | bytes 786464 | tf_op jit(solution)/shard_map/ppermute | solution.py:17
  74.9 1.8 fusion.36
  78.5 1.5 fusion.77
  82.7 4.7 %collective-permute-done.9 = f32[256,768]{1,0:T(8,128)S(1)} collective-permute-done((f32[256,768]{1,0:T(8,128)S(1)}, f32[256,768]{1,0:T(8,128)S(1)}, u32[]{:S(2)}, u32[]{:S(2)}) %collective-permute-start.9) | collective-permute-done | bytes 786464 | tf_op jit(solution)/shard_map/ppermute | solution.py:17
  88.8 7.1 %collective-permute-done.7 = bf16[256,1536]{1,0:T(8,128)(2,1)S(1)} collective-permute-done((bf16[256,1536]{1,0:T(8,128)(2,1)}, bf16[256,1536]{1,0:T(8,128)(2,1)S(1)}, u32[]{:S(2)}, u32[]{:S(2)}) %collective-permute-start.7) | collective-permute-done | bytes 786464 | tf_op jit(solution)/shard_map/ppermute | solution.py:17
  98.7 2.3 multiply_convert_fusion
  102.5 2.0 collective-permute-done.10
  106.1 11.0 %collective-permute-done.11 = f32[256,768]{1,0:T(8,128)S(1)} collective-permute-done((f32[256,768]{1,0:T(8,128)S(1)}, f32[256,768]{1,0:T(8,128)S(1)}, u32[]{:S(2)}, u32[]{:S(2)}) %collective-permute-start.11) | collective-permute-done | bytes 786464 | tf_op jit(solution)/shard_map/ppermute | solution.py:17
  118.1 18.6 %collective-permute-start.12 = (f32[256,768]{1,0:T(8,128)}, f32[256,768]{1,0:T(8,128)S(1)}, u32[]{:S(2)}, u32[]{:S(2)}) collective-permute-start(f32[256,768]{1,0:T(8,128)} %add.159), channel_id=1, source_target_pairs={{6,0},{8,2},{10,4},{12,6},{14,8},{16,10},{18,12},{20,14},{22,16},{... | collective-permute-start | bytes 2359304 | tf_op jit(solution)/shard_map/ppermute | solution.py:17
  138.0 1.8 fusion.69
  139.8 2.1 add_bitcast_fusion.1
  142.0 5.8 %collective-permute-done.12 = f32[256,768]{1,0:T(8,128)S(1)} collective-permute-done((f32[256,768]{1,0:T(8,128)}, f32[256,768]{1,0:T(8,128)S(1)}, u32[]{:S(2)}, u32[]{:S(2)}) %collective-permute-start.12) | collective-permute-done | bytes 786464 | tf_op jit(solution)/shard_map/ppermute | solution.py:17
  148.7 2.1 add_bitcast_fusion
  150.8 271.2 %all-reduce.3.cloned.1.call-done = (f32[768,768]{0,1:T(8,128)}, f32[768,768]{0,1:T(8,128)}) async-done(((f32[768,768]{0,1:T(8,128)}, f32[768,768]{0,1:T(8,128)}), (f32[768,768]{0,1:T(8,128)}, f32[768,768]{0,1:T(8,128)})) %all-reduce.3.cloned.1.call-update) | async-done | bytes 4718608 | tf_op jit(solution)/shard_map/psum | solution.py:104
  422.0 3.2 copy.14
  425.1 1.9 copy.15
  (89 shorter events, 23.5 us)
Async XLA Ops:
  7.2 8.5 %copy-start = (bf16[768,768]{1,0:T(8,128)(2,1)S(1)}, bf16[768,768]{1,0:T(8,128)(2,1)}, u32[]{:S(2)}) copy-start(bf16[768,768]{1,0:T(8,128)(2,1)} %param.14) | copy-start | bytes 3538948
  7.2 54.7 %all-gather.3.cloned.1.call-start = ((), (), s32[]{:S(2)}) async-start(), calls=%async_computation.1 | async-start | bytes 2359296 | tf_op jit(solution)/shard_map/all_gather | solution.py:78
  12.5 124.2 %reduce-scatter.2.cloned.1.call-start = ((), (), s32[]{:S(2)}) async-start(), calls=%async_computation.2 | async-start | bytes 1179648 | tf_op jit(solution)/shard_map/reduce_scatter | solution.py:100
  12.6 41.9 %copy-start.16 = (bf16[256]{0:T(256)(128)(2,1)}, bf16[256]{0:T(256)(128)(2,1)S(1)}, u32[]{:S(2)}) copy-start(bf16[256]{0:T(256)(128)(2,1)S(1)} %convert_element_type.63) | copy-start | bytes 1540
  12.6 41.1 %collective-permute-start.2 = (bf16[256]{0:T(256)(128)(2,1)S(1)}, bf16[256]{0:T(256)(128)(2,1)}, u32[]{:S(2)}, u32[]{:S(2)}) collective-permute-start(bf16[256]{0:T(256)(128)(2,1)S(1)} %convert_element_type.63), channel_id=1, source_target_pairs={{254,0},{0,2},{2,4},{4,6},{6,8},{8,10},{10,12},{12,14},{14,16},{16... | collective-permute-start | bytes 1544 | tf_op jit(solution)/shard_map/ppermute | solution.py:17
  14.1 46.8 %collective-permute-start.1 = (bf16[256,1536]{1,0:T(8,128)(2,1)}, bf16[256,1536]{1,0:T(8,128)(2,1)}, u32[]{:S(2)}, u32[]{:S(2)}) collective-permute-start(bf16[256,1536]{1,0:T(8,128)(2,1)} %fusion.1), channel_id=1, source_target_pairs={{254,0},{0,2},{2,4},{4,6},{6,8},{8,10},{10,12},{12,14},{14,16},{16... | collective-permute-start | bytes 2359304 | tf_op jit(solution)/shard_map/ppermute | solution.py:17
  16.4 36.0 %copy-start.3 = (bf16[256,768]{1,0:T(8,128)(2,1)}, bf16[256,768]{1,0:T(8,128)(2,1)S(1)}, u32[]{:S(2)}) copy-start(bf16[256,768]{1,0:T(8,128)(2,1)S(1)} %fusion.73) | copy-start | bytes 1179652
  16.4 13.6 %collective-permute-start = (bf16[256,768]{1,0:T(8,128)(2,1)S(1)}, bf16[256,768]{1,0:T(8,128)(2,1)}, u32[]{:S(2)}, u32[]{:S(2)}) collective-permute-start(bf16[256,768]{1,0:T(8,128)(2,1)S(1)} %fusion.73), channel_id=1, source_target_pairs={{254,0},{0,2},{2,4},{4,6},{6,8},{8,10},{10,12},{12,14},{14,16},{16... | collective-permute-start | bytes 1179656 | tf_op jit(solution)/shard_map/ppermute | solution.py:17
  30.1 31.7 %collective-permute-start.3 = (bf16[256,768]{1,0:T(8,128)(2,1)}, bf16[256,768]{1,0:T(8,128)(2,1)}, u32[]{:S(2)}, u32[]{:S(2)}) collective-permute-start(bf16[256,768]{1,0:T(8,128)(2,1)} %collective-permute-done), channel_id=1, source_target_pairs={{254,0},{0,2},{2,4},{4,6},{6,8},{8,10},{10,12},{12,14},{14,16},{16... | collective-permute-start | bytes 1179656 | tf_op jit(solution)/shard_map/ppermute | solution.py:17
  53.6 7.2 %collective-permute-start.5 = (bf16[256]{0:T(256)(128)(2,1)}, bf16[256]{0:T(256)(128)(2,1)}, u32[]{:S(2)}, u32[]{:S(2)}) collective-permute-start(bf16[256]{0:T(256)(128)(2,1)} %collective-permute-done.2), channel_id=1, source_target_pairs={{254,0},{0,2},{2,4},{4,6},{6,8},{8,10},{10,12},{12,14},{14,16},{16... | collective-permute-start | bytes 1544 | tf_op jit(solution)/shard_map/ppermute | solution.py:17
  60.9 27.9 %collective-permute-start.8 = (bf16[256]{0:T(256)(128)(2,1)}, bf16[256]{0:T(256)(128)(2,1)S(1)}, u32[]{:S(2)}, u32[]{:S(2)}) collective-permute-start(bf16[256]{0:T(256)(128)(2,1)} %collective-permute-done.5), channel_id=1, source_target_pairs={{254,0},{0,2},{2,4},{4,6},{6,8},{8,10},{10,12},{12,14},{14,16},{16... | collective-permute-start | bytes 1544 | tf_op jit(solution)/shard_map/ppermute | solution.py:17
  60.9 14.1 %collective-permute-start.4 = (bf16[256,1536]{1,0:T(8,128)(2,1)}, bf16[256,1536]{1,0:T(8,128)(2,1)}, u32[]{:S(2)}, u32[]{:S(2)}) collective-permute-start(bf16[256,1536]{1,0:T(8,128)(2,1)} %collective-permute-done.1), channel_id=1, source_target_pairs={{254,0},{0,2},{2,4},{4,6},{6,8},{8,10},{10,12},{12,14},{14,16},{16... | collective-permute-start | bytes 2359304 | tf_op jit(solution)/shard_map/ppermute | solution.py:17
  61.7 34.8 %collective-permute-start.6 = (bf16[256,768]{1,0:T(8,128)(2,1)}, bf16[256,768]{1,0:T(8,128)(2,1)}, u32[]{:S(2)}, u32[]{:S(2)}) collective-permute-start(bf16[256,768]{1,0:T(8,128)(2,1)} %collective-permute-done.3), channel_id=1, source_target_pairs={{254,0},{0,2},{2,4},{4,6},{6,8},{8,10},{10,12},{12,14},{14,16},{16... | collective-permute-start | bytes 1179656 | tf_op jit(solution)/shard_map/ppermute | solution.py:17
  64.3 3.5 copy-start.4
  64.7 3.5 copy-start.14
  64.7 22.8 %collective-permute-start.9 = (f32[256,768]{1,0:T(8,128)S(1)}, f32[256,768]{1,0:T(8,128)S(1)}, u32[]{:S(2)}, u32[]{:S(2)}) collective-permute-start(f32[256,768]{1,0:T(8,128)S(1)} %convolution_multiply_fusion.3), channel_id=1, source_target_pairs={{254,0},{0,2},{2,4},{4,6},{6,8},{8,10},{10,12},{12,14},{14,16},{16... | collective-permute-start | bytes 2359304 | tf_op jit(solution)/shard_map/ppermute | solution.py:17
  76.7 19.2 %collective-permute-start.7 = (bf16[256,1536]{1,0:T(8,128)(2,1)}, bf16[256,1536]{1,0:T(8,128)(2,1)S(1)}, u32[]{:S(2)}, u32[]{:S(2)}) collective-permute-start(bf16[256,1536]{1,0:T(8,128)(2,1)} %collective-permute-done.4), channel_id=1, source_target_pairs={{254,0},{0,2},{2,4},{4,6},{6,8},{8,10},{10,12},{12,14},{14,16},{16... | collective-permute-start | bytes 2359304 | tf_op jit(solution)/shard_map/ppermute | solution.py:17
  78.5 10.3 %copy-start.6 = (bf16[512,256]{1,0:T(8,128)(2,1)}, bf16[512,256]{1,0:T(8,128)(2,1)S(1)}, u32[]{:S(2)}) copy-start(bf16[512,256]{1,0:T(8,128)(2,1)S(1)} %fusion.60) | copy-start | bytes 786436
  88.7 15.7 %collective-permute-start.10 = (f32[256,768]{1,0:T(8,128)}, f32[256,768]{1,0:T(8,128)}, u32[]{:S(2)}, u32[]{:S(2)}) collective-permute-start(f32[256,768]{1,0:T(8,128)} %fusion.2), channel_id=1, source_target_pairs={{254,0},{0,2},{2,4},{4,6},{6,8},{8,10},{10,12},{12,14},{14,16},{16... | collective-permute-start | bytes 2359304 | tf_op jit(solution)/shard_map/ppermute | solution.py:17
  101.0 320.9 %all-reduce.3.cloned.1.call-start = ((), (), s32[]{:S(2)}) async-start(), calls=%async_computation.3 | async-start | bytes 9437184 | tf_op jit(solution)/shard_map/psum | solution.py:104
  102.4 3.3 copy-start.8
  105.7 11.5 %collective-permute-start.11 = (f32[256,768]{1,0:T(8,128)S(1)}, f32[256,768]{1,0:T(8,128)S(1)}, u32[]{:S(2)}, u32[]{:S(2)}) collective-permute-start(f32[256,768]{1,0:T(8,128)S(1)} %add.158), channel_id=1, source_target_pairs={{254,0},{0,2},{2,4},{4,6},{6,8},{8,10},{10,12},{12,14},{14,16},{16... | collective-permute-start | bytes 2359304 | tf_op jit(solution)/shard_map/ppermute | solution.py:17
  118.1 29.6 %collective-permute-start.12 = (f32[256,768]{1,0:T(8,128)}, f32[256,768]{1,0:T(8,128)S(1)}, u32[]{:S(2)}, u32[]{:S(2)}) collective-permute-start(f32[256,768]{1,0:T(8,128)} %add.159), channel_id=1, source_target_pairs={{6,0},{8,2},{10,4},{12,6},{14,8},{16,10},{18,12},{20,14},{22,16},{... | collective-permute-start | bytes 2359304 | tf_op jit(solution)/shard_map/ppermute | solution.py:17
  142.0 6.0 %copy-start.13 = (bf16[256,768]{1,0:T(8,128)(2,1)S(1)}, bf16[256,768]{1,0:T(8,128)(2,1)}, u32[]{:S(2)}) copy-start(bf16[256,768]{1,0:T(8,128)(2,1)} %param.12) | copy-start | bytes 1179652
  (9 other events, 18.2 us)
Sparse Core Ops, SparseCore 0:
  12.6 45.1 all-gather.2
  101.2 28.7 reduce-scatter.1
  150.9 271.0 all-reduce.2
where the time goes:
time: 434 us
  waiting for transfers between devices  320 us (74%)
  matrix products  33 us (8%)
  blocking collectives  28.1 us (6%)
  starting transfers between devices  25.8 us (6%)
  between operations  14.1 us (3%)
  other arithmetic  6.48 us (1%)
  local copies, waits for them, and re-layouts  5.91 us (1%)
    psum x1, waiting for transfers between devices, local(): lax.psum((image_part, text_part), ('dp', 'section'))  271 us
    ppermute x13, waiting for transfers between devices, passed_along(): return lax.ppermute(block, axis, route)  49 us
    ppermute x13, starting transfers between devices, passed_along(): return lax.ppermute(block, axis, route)  25.7 us
    all_gather x1, blocking collectives, local(): lax.all_gather(image_emb, 'section', axis=0, tiled=True)  22.3 us
  transfers between devices with their start and end apart: 16, of which 9 were waited for; matrix products, arithmetic and copies ran while one was open for 7% of the time, Pallas kernels for 0%

commit v1 on v0

--- a/solution.py
+++ b/solution.py
@@ -101,7 +101,7 @@
         grad_rows.astype(jnp.bfloat16), "section", scatter_dimension=0, tiled=True
     ).astype(jnp.float32)
     image_part = weight_grad(image_feats, image_unit, image_len, own_grads)
-    image_total, text_total = lax.psum((image_part, text_part), ("dp", "section"))
+    image_total, text_total = lax.psum(lax.psum((image_part, text_part), "section"), "dp")
     return (image_total, text_total)
 
 

time: 434 us -> 1390 us (3.20)
  waiting for transfers between devices: 320 us -> 1270 us
    psum x1 -> x2, waiting for transfers between devices: 271 us -> 1220 us  [the longest x1 1080 us: local(): lax.psum(lax.psum((image_part, text_part), 'section'), 'dp')]
  transfers between devices with their start and end apart: 16 -> 17, of which waited for: 9 -> 10; matrix products, arithmetic and copies ran while one was open for 7% -> 2% of each run, Pallas kernels for 0% -> 0%
where the time goes in v1:
time: 1390 us; the launch traced here: 1380 us
  waiting for transfers between devices  1270 us (91%)
  matrix products  33 us (2%)
  blocking collectives  28.1 us (2%)
  starting transfers between devices  25.8 us (2%)
  between operations  14.1 us (1%)
    psum x1, waiting for transfers between devices, local(): lax.psum(lax.psum((image_part, text_part), 'section'), 'dp')  1080 us
    psum x1, waiting for transfers between devices, local(): lax.psum((image_part, text_part), 'section')  133 us
    ppermute x13, waiting for transfers between devices, passed_along(): return lax.ppermute(block, axis, route)  49 us
  transfers between devices with their start and end apart: 17, of which 10 were waited for; matrix products, arithmetic and copies ran while one was open for 2% of the time, Pallas kernels for 0%

profile of v1, /device:TPU:2, one launch (start us, length us, event | category | flops | bytes accessed | tf_op | source)
XLA Modules:
  0.0 1378.9 jit_solution(17376942863826828389)
XLA Ops:
  7.2 4.1 multiply_reduce_fusion
  14.1 1.6 collective-permute-start.1
  17.2 12.8 collective-permute-done
  30.1 22.3 %all_gather.9 = bf16[512,768]{1,0:T(8,128)(2,1)S(1)} all-gather(bf16[256,768]{1,0:T(8,128)(2,1)S(1)} %fusion.74), channel_id=1, replica_groups=mesh['dp'=128,'section'=2] {'section'}, dimensions={0}, use_global_device_ids=true | all-gather | bytes 1179648 | tf_op jit(solution)/shard_map/all_gather | solution.py:79
  54.5 5.7 all-gather
  61.8 2.4 fusion.62
  64.7 3.1 collective-permute-start.9
  68.2 1.8 fusion.43
  70.0 4.9 collective-permute-done.4
  74.9 1.8 fusion.36
  82.7 4.7 collective-permute-done.9
  88.8 7.1 collective-permute-done.7
  98.7 2.3 multiply_convert_fusion
  102.5 2.0 collective-permute-done.10
  106.1 11.0 collective-permute-done.11
  118.1 18.9 %collective-permute-start.12 = (f32[256,768]{1,0:T(8,128)}, f32[256,768]{1,0:T(8,128)S(1)}, u32[]{:S(2)}, u32[]{:S(2)}) collective-permute-start(f32[256,768]{1,0:T(8,128)} %add.163), channel_id=1, source_target_pairs={{6,0},{8,2},{10,4},{12,6},{14,8},{16,10},{18,12},{20,14},{22,16},{... | collective-permute-start | bytes 2359304 | tf_op jit(solution)/shard_map/ppermute | solution.py:17
  138.3 1.8 fusion.69
  140.2 2.1 add_bitcast_fusion.1
  142.3 5.5 collective-permute-done.12
  148.7 2.1 add_bitcast_fusion
  150.8 132.7 %all-reduce.7.cloned.1.call-done = (f32[768,768]{0,1:T(8,128)}, f32[768,768]{0,1:T(8,128)}) async-done(((f32[768,768]{0,1:T(8,128)}, f32[768,768]{0,1:T(8,128)}), (f32[768,768]{0,1:T(8,128)}, f32[768,768]{0,1:T(8,128)})) %all-reduce.7.cloned.1.call-update) | async-done | bytes 4718608 | tf_op jit(solution)/shard_map/psum | solution.py:104
  283.5 1083.7 %all-reduce.5.cloned.1.call-done = (f32[768,768]{0,1:T(8,128)}, f32[768,768]{0,1:T(8,128)}) async-done(((f32[768,768]{0,1:T(8,128)}, f32[768,768]{0,1:T(8,128)}), (f32[768,768]{0,1:T(8,128)}, f32[768,768]{0,1:T(8,128)})) %all-reduce.5.cloned.1.call-update) | async-done | bytes 4718608 | tf_op jit(solution)/shard_map/psum | solution.py:104
  1367.2 3.2 copy.14
  1370.4 1.9 copy.15
  (92 shorter events, 25.0 us)
Async XLA Ops:
  7.2 8.5 copy-start
  7.2 54.7 %all-gather.3.cloned.1.call-start = ((), (), s32[]{:S(2)}) async-start(), calls=%async_computation.1 | async-start | bytes 2359296 | tf_op jit(solution)/shard_map/all_gather | solution.py:78
  12.5 124.5 %reduce-scatter.2.cloned.1.call-start = ((), (), s32[]{:S(2)}) async-start(), calls=%async_computation.2 | async-start | bytes 1179648 | tf_op jit(solution)/shard_map/reduce_scatter | solution.py:100
  12.6 41.9 %copy-start.16 = (bf16[256]{0:T(256)(128)(2,1)}, bf16[256]{0:T(256)(128)(2,1)S(1)}, u32[]{:S(2)}) copy-start(bf16[256]{0:T(256)(128)(2,1)S(1)} %convert_element_type.63) | copy-start | bytes 1540
  12.6 41.1 %collective-permute-start.2 = (bf16[256]{0:T(256)(128)(2,1)S(1)}, bf16[256]{0:T(256)(128)(2,1)}, u32[]{:S(2)}, u32[]{:S(2)}) collective-permute-start(bf16[256]{0:T(256)(128)(2,1)S(1)} %convert_element_type.63), channel_id=1, source_target_pairs={{254,0},{0,2},{2,4},{4,6},{6,8},{8,10},{10,12},{12,14},{14,16},{16... | collective-permute-start | bytes 1544 | tf_op jit(solution)/shard_map/ppermute | solution.py:17
  14.1 47.1 %collective-permute-start.1 = (bf16[256,1536]{1,0:T(8,128)(2,1)}, bf16[256,1536]{1,0:T(8,128)(2,1)}, u32[]{:S(2)}, u32[]{:S(2)}) collective-permute-start(bf16[256,1536]{1,0:T(8,128)(2,1)} %fusion.1), channel_id=1, source_target_pairs={{254,0},{0,2},{2,4},{4,6},{6,8},{8,10},{10,12},{12,14},{14,16},{16... | collective-permute-start | bytes 2359304 | tf_op jit(solution)/shard_map/ppermute | solution.py:17
  16.4 36.0 %copy-start.3 = (bf16[256,768]{1,0:T(8,128)(2,1)}, bf16[256,768]{1,0:T(8,128)(2,1)S(1)}, u32[]{:S(2)}) copy-start(bf16[256,768]{1,0:T(8,128)(2,1)S(1)} %fusion.73) | copy-start | bytes 1179652
  16.4 13.6 collective-permute-start
  30.1 31.7 %collective-permute-start.3 = (bf16[256,768]{1,0:T(8,128)(2,1)}, bf16[256,768]{1,0:T(8,128)(2,1)}, u32[]{:S(2)}, u32[]{:S(2)}) collective-permute-start(bf16[256,768]{1,0:T(8,128)(2,1)} %collective-permute-done), channel_id=1, source_target_pairs={{254,0},{0,2},{2,4},{4,6},{6,8},{8,10},{10,12},{12,14},{14,16},{16... | collective-permute-start | bytes 1179656 | tf_op jit(solution)/shard_map/ppermute | solution.py:17
  53.6 7.5 collective-permute-start.5
  61.2 27.6 %collective-permute-start.8 = (bf16[256]{0:T(256)(128)(2,1)}, bf16[256]{0:T(256)(128)(2,1)S(1)}, u32[]{:S(2)}, u32[]{:S(2)}) collective-permute-start(bf16[256]{0:T(256)(128)(2,1)} %collective-permute-done.5), channel_id=1, source_target_pairs={{254,0},{0,2},{2,4},{4,6},{6,8},{8,10},{10,12},{12,14},{14,16},{16... | collective-permute-start | bytes 1544 | tf_op jit(solution)/shard_map/ppermute | solution.py:17
  61.2 13.8 collective-permute-start.4
  61.7 34.8 %collective-permute-start.6 = (bf16[256,768]{1,0:T(8,128)(2,1)}, bf16[256,768]{1,0:T(8,128)(2,1)}, u32[]{:S(2)}, u32[]{:S(2)}) collective-permute-start(bf16[256,768]{1,0:T(8,128)(2,1)} %collective-permute-done.3), channel_id=1, source_target_pairs={{254,0},{0,2},{2,4},{4,6},{6,8},{8,10},{10,12},{12,14},{14,16},{16... | collective-permute-start | bytes 1179656 | tf_op jit(solution)/shard_map/ppermute | solution.py:17
  64.3 3.5 copy-start.4
  64.7 3.5 copy-start.14
  64.7 22.8 %collective-permute-start.9 = (f32[256,768]{1,0:T(8,128)S(1)}, f32[256,768]{1,0:T(8,128)S(1)}, u32[]{:S(2)}, u32[]{:S(2)}) collective-permute-start(f32[256,768]{1,0:T(8,128)S(1)} %convolution_multiply_fusion.3), channel_id=1, source_target_pairs={{254,0},{0,2},{2,4},{4,6},{6,8},{8,10},{10,12},{12,14},{14,16},{16... | collective-permute-start | bytes 2359304 | tf_op jit(solution)/shard_map/ppermute | solution.py:17
  76.7 19.2 %collective-permute-start.7 = (bf16[256,1536]{1,0:T(8,128)(2,1)}, bf16[256,1536]{1,0:T(8,128)(2,1)S(1)}, u32[]{:S(2)}, u32[]{:S(2)}) collective-permute-start(bf16[256,1536]{1,0:T(8,128)(2,1)} %collective-permute-done.4), channel_id=1, source_target_pairs={{254,0},{0,2},{2,4},{4,6},{6,8},{8,10},{10,12},{12,14},{14,16},{16... | collective-permute-start | bytes 2359304 | tf_op jit(solution)/shard_map/ppermute | solution.py:17
  78.5 10.3 copy-start.6
  88.7 15.7 %collective-permute-start.10 = (f32[256,768]{1,0:T(8,128)}, f32[256,768]{1,0:T(8,128)}, u32[]{:S(2)}, u32[]{:S(2)}) collective-permute-start(f32[256,768]{1,0:T(8,128)} %fusion.2), channel_id=1, source_target_pairs={{254,0},{0,2},{2,4},{4,6},{6,8},{8,10},{10,12},{12,14},{14,16},{16... | collective-permute-start | bytes 2359304 | tf_op jit(solution)/shard_map/ppermute | solution.py:17
  101.1 182.5 %all-reduce.7.cloned.1.call-start = ((), (), s32[]{:S(2)}) async-start(), calls=%async_computation.4 | async-start | bytes 9437184 | tf_op jit(solution)/shard_map/psum | solution.py:104
  105.7 11.5 collective-permute-start.11
  118.1 29.6 %collective-permute-start.12 = (f32[256,768]{1,0:T(8,128)}, f32[256,768]{1,0:T(8,128)S(1)}, u32[]{:S(2)}, u32[]{:S(2)}) collective-permute-start(f32[256,768]{1,0:T(8,128)} %add.163), channel_id=1, source_target_pairs={{6,0},{8,2},{10,4},{12,6},{14,8},{16,10},{18,12},{20,14},{22,16},{... | collective-permute-start | bytes 2359304 | tf_op jit(solution)/shard_map/ppermute | solution.py:17
  142.3 5.7 copy-start.13
  150.8 1216.5 %all-reduce.5.cloned.1.call-start = ((), (), s32[]{:S(2)}) async-start(), calls=%async_computation.3 | async-start | bytes 9437184 | tf_op jit(solution)/shard_map/psum | solution.py:104
  (10 other events, 21.5 us)
Sparse Core Ops, SparseCore 0:
  12.6 45.1 all-gather.2
  101.2 29.0 reduce-scatter.1
  150.9 132.6 all-reduce.6
  286.1 1081.0 all-reduce.4
